TPU v7x, 32 devices: a whole 2x2x4 slice. The times are simulated.
32 devices in a mesh: seq: 8 (over y, x, core), head: 4 (over z).
Axes of the slice: x: 2, y: 2, z: 4, core: 2. Of those that a mesh axis runs over, the one named last changes fastest.
Arguments:
- queries: bfloat16 [16384, 512], P('seq', 'head'), may hold values from -4 to 4
- key_rows: bfloat16 [16384, 512], P('seq', 'head'), may hold values from -4 to 4
- value_rows: bfloat16 [16384, 512], P('seq', 'head'), may hold values from -6 to 6
- norm_gain: float32 [512], P('head'), may hold values from 0.1 to 1.9
- out_grad: bfloat16 [16384, 512], P('seq', 'head'), may hold values from -6 to 6
Outputs:
- normed: bfloat16 [16384, 512], P('seq', 'head')
- query_grad: bfloat16 [16384, 512], P('seq', 'head')
- key_grad: bfloat16 [16384, 512], P('seq', 'head')
- value_grad: bfloat16 [16384, 512], P('seq', 'head')
All inputs are finite; a program needn't handle non-finite values.
Results may differ from a plain program's by a relative error of at most 0.0059.
Values sent between devices are 32-bit elements; how exact they have to be, the bound alone decides.
A program may use at most 64 MiB of HBM per device.

v0:
```python
import jax
import jax.numpy as jnp
from jax import lax
from jax.sharding import PartitionSpec as P

HEAD_DIM = 128
BLOCK = 512


def causal_mask(size):
    row_index = lax.broadcasted_iota(jnp.int32, (size, size), 0)
    col_index = lax.broadcasted_iota(jnp.int32, (size, size), 1)
    return row_index >= col_index


def body(queries, key_rows, value_rows, norm_gain, out_grad):
    tokens_here = queries.shape[0]
    heads_here = queries.shape[1] // HEAD_DIM
    blocks = tokens_here // BLOCK
    block_shape = (blocks, BLOCK, heads_here, HEAD_DIM)
    query4 = queries.reshape(block_shape)
    key4 = key_rows.reshape(block_shape)
    value4 = value_rows.reshape(block_shape)
    width_all = heads_here * HEAD_DIM * lax.axis_size("head")
    mask4 = causal_mask(BLOCK)[None, None]
    position = lax.axis_index("seq")
    states = jnp.einsum("bshd,bshe->bhde", key4, value4, preferred_element_type=jnp.float32)
    totals = jnp.sum(states, 0)
    piece = lax.all_gather(totals[None], "seq", axis=0, tiled=True)
    anchor = jnp.arange(piece.shape[0], dtype=jnp.int32)
    keep = (anchor < position)[:, None, None, None]
    earlier = jnp.sum(jnp.where(keep, piece, 0.0), 0)
    running = jnp.cumsum(states, 0)
    within = jnp.concatenate([jnp.zeros_like(states[:1]), running[:-1]], 0)
    prefix16 = (earlier[None] + within).astype(jnp.bfloat16)
    scores = jnp.einsum("bthd,bshd->bhts", query4, key4, preferred_element_type=jnp.float32)
    attn = jnp.where(mask4, scores, 0.0).astype(jnp.bfloat16)
    output = jnp.einsum("bhts,bshe->bthe", attn, value4, preferred_element_type=jnp.float32)
    output = output + jnp.einsum(
        "bthd,bhde->bthe", query4, prefix16, preferred_element_type=jnp.float32
    )
    gain4 = norm_gain.reshape(heads_here, HEAD_DIM)
    scaled = out_grad.reshape(block_shape).astype(jnp.float32) * gain4
    squares, products = lax.psum(
        (jnp.sum(output * output, (2, 3)), jnp.sum(scaled * output, (2, 3))), "head"
    )
    rstd = lax.rsqrt(squares / width_all + 1e-05)[:, :, None, None]
    normed = (output * rstd * gain4).astype(jnp.bfloat16).reshape(tokens_here, -1)
    mean_prod = (products / width_all)[:, :, None, None]
    dout = (rstd * scaled - output * rstd**3 * mean_prod).astype(jnp.bfloat16)
    grad_states = jnp.einsum("bthd,bthe->bhde", query4, dout, preferred_element_type=jnp.float32)
    grad_total = jnp.sum(grad_states, 0)
    piece = lax.all_gather(grad_total[None], "seq", axis=0, tiled=True)
    anchor = jnp.arange(piece.shape[0], dtype=jnp.int32)
    keep = (anchor > position)[:, None, None, None]
    later = jnp.sum(jnp.where(keep, piece, 0.0), 0)
    behind = jnp.cumsum(grad_states[::-1], 0)[::-1]
    after = jnp.concatenate([behind[1:], jnp.zeros_like(grad_states[:1])], 0)
    suffix16 = (later[None] + after).astype(jnp.bfloat16)
    bmat = jnp.einsum("bthe,bshe->bhts", dout, value4, preferred_element_type=jnp.float32)
    bmat = jnp.where(mask4, bmat, 0.0).astype(jnp.bfloat16)
    query_grad = jnp.einsum("bhts,bshd->bthd", bmat, key4, preferred_element_type=jnp.float32)
    query_grad = query_grad + jnp.einsum(
        "bthe,bhde->bthd", dout, prefix16, preferred_element_type=jnp.float32
    )
    key_grad = jnp.einsum("bhts,bthd->bshd", bmat, query4, preferred_element_type=jnp.float32)
    key_grad = key_grad + jnp.einsum(
        "bshe,bhde->bshd", value4, suffix16, preferred_element_type=jnp.float32
    )
    value_grad = jnp.einsum("bhts,bthe->bshe", attn, dout, preferred_element_type=jnp.float32)
    value_grad = value_grad + jnp.einsum(
        "bshd,bhde->bshe", key4, suffix16, preferred_element_type=jnp.float32
    )
    return (
        normed,
        query_grad.astype(jnp.bfloat16).reshape(tokens_here, -1),
        key_grad.astype(jnp.bfloat16).reshape(tokens_here, -1),
        value_grad.astype(jnp.bfloat16).reshape(tokens_here, -1),
    )


def solution(mesh):
    return jax.shard_map(
        body,
        mesh=mesh,
        in_specs=(
            P("seq", "head"),
            P("seq", "head"),
            P("seq", "head"),
            P("head"),
            P("seq", "head"),
        ),
        out_specs=(P("seq", "head"), P("seq", "head"), P("seq", "head"), P("seq", "head")),
        check_vma=False,
    )
```

profile of v0, /device:TPU:0, one launch (start us, length us, event | category | flops | bytes accessed | tf_op | source)
XLA Modules:
  0.0 71.4 jit_solution(403312878023820120)
XLA Ops:
  0.6 0.0 copy-start
  0.6 0.0 copy-start.1
  0.7 1.0 %copy-done = bf16[2048,128]{1,0:T(8,128)(2,1)S(1)} copy-done((bf16[2048,128]{1,0:T(8,128)(2,1)S(1)}, bf16[2048,128]{1,0:T(8,128)(2,1)}, u32[]{:S(2)}) %copy-start) | copy-done | bytes 524312
  1.7 0.1 iota_compare_fusion
  1.8 0.0 copy-start.9
  1.8 1.9 %select_convert_fusion.1 = bf16[4,512,512]{2,1,0:T(8,128)(2,1)S(1)} fusion(bf16[4,512,128]{2,1,0:T(8,128)(2,1)S(1)} %bitcast.81, bf16[4,512,128]{2,1,0:T(8,128)(2,1)} %bitcast.89, pred[512,512]{1,0:T(8,128)(4,1)S(1)} %iota_compare_fusion), kind=kOutput, calls=%fused_computation.1 | convolution fusion | flops 270532608 | bytes 3407872 | tf_op jit(solution)/shard_map/bthd,bshd->bhts/dot_general | solution.py:36
  3.7 0.0 copy-start.3
  3.7 0.0 copy-done.1
  3.7 1.7 %convolution_bitcast_fusion.2 = f32[4,128,512]{1,2,0:T(8,128)} fusion(bf16[4,512,512]{2,1,0:T(8,128)(2,1)S(1)} %select_convert_fusion.1, bf16[4,512,128]{2,1,0:T(8,128)(2,1)S(1)} %bitcast.85), kind=kOutput, calls=%fused_computation.4 | convolution fusion | flops 268435456 | bytes 3670016 | tf_op jit(solution)/shard_map/bhts,bshe->bthe/dot_general | solution.py:38
  5.4 0.0 copy-done.9
  5.4 0.0 copy-done.3
  5.4 0.0 copy-start.10
  5.4 0.3 fusion.26
  5.7 12.4 %all-gather = f32[1024,128]{1,0:T(8,128)} all-gather(f32[128,128]{1,0:T(8,128)S(1)} %get-tuple-element.12), channel_id=2, replica_groups=mesh['seq'=8,'head'=4] {'seq'}, dimensions={0}, use_global_device_ids=true | all-gather | bytes 589824 | tf_op jit(solution)/shard_map/all_gather | solution.py:29
  18.1 1.3 %copy.39 = f32[8,1,128,128]{2,0,3,1:T(8,128)S(1)} copy(f32[8,1,128,128]{3,2,0,1:T(8,128)} %bitcast.93) | data formatting | bytes 1048576 | tf_op jit(solution)/shard_map/all_gather | solution.py:29
  19.4 0.2 select_reduce_fusion
  19.6 0.1 copy.40
  19.7 0.0 copy-start.6
  19.7 0.2 fusion.14
  19.9 0.0 copy-done.10
  19.9 2.8 %fusion.9 = (f32[4,512]{1,0:T(4,128)S(1)}, f32[4,512]{1,0:T(4,128)S(1)}, f32[4,512,1,128]{3,1,0,2:T(8,128)}) fusion(bf16[4,512,1,128]{3,1,0,2:T(8,128)(2,1)} %bitcast.95, f32[128]{0:T(128)S(1)} %copy-done.10, f32[4,128,512]{1,2,0:T(8,128)} %convolution_bitcast_fusion.2, bf16[4,512,128]{2,1,0:T(8,128)(2,1)S(1)} %bitcast.82, ...), kind=kOutput, calls=%fused_computation.20 | convolution fusion | flops 69070848 | bytes 3424768 | tf_op jit(solution)/shard_map/bthd,bhde->bthe/dot_general | solution.py:39
  22.7 0.0 copy-done.6
  22.7 19.0 %all-reduce.2 = (f32[4,512]{1,0:T(4,128)S(1)}, f32[4,512]{1,0:T(4,128)S(1)}) all-reduce(f32[4,512]{1,0:T(4,128)S(1)} %get-tuple-element.5, f32[4,512]{1,0:T(4,128)S(1)} %get-tuple-element.4), channel_id=1, replica_groups=mesh['seq'=8,'head'=4] {'head'}, use_global_device_ids=true, to_apply=%region_4.5 | all-reduce | flops 4096 | bytes 32768 | tf_op jit(solution)/shard_map/psum | solution.py:44
  41.7 2.8 %fusion.10 = (bf16[4,512,128]{2,1,0:T(8,128)(2,1)S(1)}, bf16[4,512,1,128]{3,1,0,2:T(8,128)(2,1)}) fusion(f32[4,512,1,128]{3,1,0,2:T(8,128)} %get-tuple-element.14, f32[4,512]{1,0:T(4,128)S(1)} %get-tuple-element.17, f32[4,512]{1,0:T(4,128)S(1)} %get-tuple-element.10, f32[128]{0:T(128)S(1)} %copy-done.10, f32[4,512]{1,0:T(4,128)S(1)} %get-tuple-element.11, ...), kind=kLoop, calls=%fused_computation.24 | loop fusion | flops 2621440 | bytes 2646528 | tf_op jit(solution)/shard_map/reshape.36
  44.5 1.5 %fusion.28 = f32[4,128,512]{2,1,0:T(8,128)} fusion(bf16[4,512,128]{2,1,0:T(8,128)(2,1)S(1)} %get-tuple-element.8, bf16[4,512,512]{2,1,0:T(8,128)(2,1)S(1)} %select_convert_fusion.1), kind=kOutput, calls=%fused_computation.47 | convolution fusion | flops 268435456 | bytes 3670016 | tf_op jit(solution)/shard_map/bhts,bthe->bshe/dot_general | solution.py:70
  46.0 1.0 %fusion.27 = (f32[128,128]{0,1:T(8,128)S(1)}, f32[4,128,128]{1,2,0:T(8,128)}) fusion(bf16[4,512,128]{2,1,0:T(8,128)(2,1)S(1)} %get-tuple-element.8, bf16[4,512,128]{2,1,0:T(8,128)(2,1)S(1)} %bitcast.84), kind=kOutput, calls=%fused_computation.46 | convolution fusion | flops 67158016 | bytes 1376256 | tf_op jit(solution)/shard_map/bthd,bthe->bhde/dot_general | solution.py:51
  47.1 0.0 copy-start.5
  47.1 11.0 %all-gather.1 = f32[1024,128]{0,1:T(8,128)S(1)} all-gather(f32[128,128]{0,1:T(8,128)S(1)} %get-tuple-element.15), channel_id=3, replica_groups=mesh['seq'=8,'head'=4] {'seq'}, dimensions={0}, use_global_device_ids=true | all-gather | bytes 589824 | tf_op jit(solution)/shard_map/all_gather | solution.py:53
  58.0 0.1 copy.59
  58.1 0.8 %fusion.11 = f32[128,128]{0,1:T(8,128)} fusion(f32[16,8,8,128]{3,2,1,0:T(8,128)S(1)} %copy.59, pred[8]{0:T(512)(128)(4,1)S(1)} %iota_compare_fusion.1), kind=kLoop, calls=%fused_computation.26 | loop fusion | flops 245760 | bytes 589832 | tf_op jit(solution)/shard_map/reduce_sum | solution.py:56
  59.0 1.0 %reverse.4 = f32[4,128,128]{1,2,0:T(8,128)S(1)} reverse(f32[4,128,128]{1,2,0:T(8,128)} %get-tuple-element.16), dimensions={0} | reverse | bytes 524288 | tf_op jit(solution)/shard_map/reverse
  59.9 0.2 fusion.12
  60.1 0.0 copy-start.2
  60.1 0.7 slice.13
  60.8 0.9 %slice.11 = f32[3,1,128,128]{2,3,0,1:T(8,128)S(1)} reverse(f32[3,1,128,128]{2,3,0,1:T(8,128)} %slice.13), dimensions={0} | reverse | bytes 393216 | tf_op jit(solution)/shard_map/slice | solution.py:58
  61.8 0.0 copy-done.4
  61.8 0.0 copy-done.5
  61.8 1.9 %fusion.4 = bf16[4,512,1,128]{1,3,0,2:T(8,128)(2,1)} fusion(f32[4,128,512]{2,1,0:T(8,128)S(1)} %copy-done.5, bf16[4,512,128]{2,1,0:T(8,128)(2,1)S(1)} %bitcast.91, f32[3,1,128,128]{2,3,0,1:T(8,128)S(1)} %slice.11, f32[128,128]{0,1:T(8,128)} %fusion.11), kind=kOutput, calls=%fused_computation.13 | convolution fusion | flops 67764224 | bytes 2359296 | tf_op jit(solution)/shard_map/bshd,bhde->bshe/dot_general | solution.py:71
  63.7 2.0 %copy.49 = bf16[4,512,1,128]{3,1,0,2:T(8,128)(2,1)} copy(bf16[4,512,1,128]{1,3,0,2:T(8,128)(2,1)} %fusion.4) | data formatting | bytes 1048576 | tf_op jit(solution)/shard_map/convert_element_type | solution.py:78
  65.8 0.0 copy-done.2
  65.8 1.7 %select_convert_fusion = bf16[4,512,512]{2,1,0:T(8,128)(2,1)S(1)} fusion(bf16[4,512,128]{2,1,0:T(8,128)(2,1)S(1)} %get-tuple-element.8, bf16[4,512,128]{2,1,0:T(8,128)(2,1)S(1)} %bitcast.87, pred[512,512]{1,0:T(8,128)(4,1)} %copy-done.9), kind=kOutput, calls=%fused_computation | convolution fusion | flops 270532608 | bytes 3407872 | tf_op jit(solution)/shard_map/bthe,bshe->bhts/dot_general | solution.py:60
  67.5 0.0 copy-start.8
  67.5 0.9 %convolution_bitcast_fusion = f32[4,128,512]{1,2,0:T(8,128)S(1)} fusion(bf16[4,512,512]{2,1,0:T(8,128)(2,1)S(1)} %select_convert_fusion, bf16[4,512,128]{2,1,0:T(8,128)(2,1)S(1)} %bitcast.83), kind=kOutput, calls=%fused_computation.2 | convolution fusion | flops 268435456 | bytes 3670016 | tf_op jit(solution)/shard_map/bhts,bthd->bshd/dot_general | solution.py:66
  68.4 0.0 copy-done.8
  68.4 1.1 %fusion.3 = bf16[4,128,512]{1,2,0:T(8,128)(2,1)} fusion(f32[4,128,512]{1,2,0:T(8,128)S(1)} %convolution_bitcast_fusion, bf16[4,512,128]{2,1,0:T(8,128)(2,1)S(1)} %bitcast.88, f32[3,1,128,128]{2,3,0,1:T(8,128)S(1)} %slice.11, f32[128,128]{0,1:T(8,128)S(1)} %copy-done.8), kind=kOutput, calls=%fused_computation.12 | convolution fusion | flops 67764224 | bytes 2359296 | tf_op jit(solution)/shard_map/bshe,bhde->bshd/dot_general | solution.py:67
  69.5 0.7 convolution_bitcast_fusion.1
  70.2 0.1 copy-done.7
  70.3 1.1 %fusion.1 = bf16[4,128,512]{1,2,0:T(8,128)(2,1)} fusion(f32[4,128,512]{1,2,0:T(8,128)S(1)} %convolution_bitcast_fusion.1, bf16[4,512,128]{2,1,0:T(8,128)(2,1)S(1)} %get-tuple-element.8, f32[3,1,128,128]{3,2,0,1:T(8,128)S(1)} %slice.12, f32[128,128]{1,0:T(8,128)S(1)} %copy-done.7), kind=kOutput, calls=%fused_computation.10 | convolution fusion | flops 67764224 | bytes 2359296 | tf_op jit(solution)/shard_map/bthe,bhde->bthd/dot_general | solution.py:63
  (6 shorter events, 0.0 us)
Async XLA Ops:
  0.6 1.0 %copy-start = (bf16[2048,128]{1,0:T(8,128)(2,1)S(1)}, bf16[2048,128]{1,0:T(8,128)(2,1)}, u32[]{:S(2)}) copy-start(bf16[2048,128]{1,0:T(8,128)(2,1)} %param.5) | copy-start | bytes 1572868
  0.6 3.0 %copy-start.1 = (bf16[2048,128]{1,0:T(8,128)(2,1)S(1)}, bf16[2048,128]{1,0:T(8,128)(2,1)}, u32[]{:S(2)}) copy-start(bf16[2048,128]{1,0:T(8,128)(2,1)} %param.7) | copy-start | bytes 1572868
  1.8 3.6 %copy-start.9 = (pred[512,512]{1,0:T(8,128)(4,1)}, pred[512,512]{1,0:T(8,128)(4,1)S(1)}, u32[]{:S(2)}) copy-start(pred[512,512]{1,0:T(8,128)(4,1)S(1)} %iota_compare_fusion) | copy-start | bytes 786436
  3.7 1.7 %copy-start.3 = (bf16[2048,128]{1,0:T(8,128)(2,1)S(1)}, bf16[2048,128]{1,0:T(8,128)(2,1)}, u32[]{:S(2)}) copy-start(bf16[2048,128]{1,0:T(8,128)(2,1)} %param.6) | copy-start | bytes 1572868
  5.4 14.5 %copy-start.10 = (f32[128]{0:T(128)S(1)}, f32[128]{0:T(128)}, u32[]{:S(2)}) copy-start(f32[128]{0:T(128)} %param.8) | copy-start | bytes 1540
  19.7 3.0 %copy-start.6 = (f32[128,128]{1,0:T(8,128)}, f32[128,128]{1,0:T(8,128)S(1)}, u32[]{:S(2)}) copy-start(f32[128,128]{1,0:T(8,128)S(1)} %copy.40) | copy-start | bytes 196612
  47.1 14.7 %copy-start.4 = (bf16[2048,128]{1,0:T(8,128)(2,1)S(1)}, bf16[2048,128]{1,0:T(8,128)(2,1)}, u32[]{:S(2)}) copy-start(bf16[2048,128]{1,0:T(8,128)(2,1)} %param.6) | copy-start | bytes 1572868
  47.1 14.7 %copy-start.5 = (f32[4,128,512]{2,1,0:T(8,128)S(1)}, f32[4,128,512]{2,1,0:T(8,128)}, u32[]{:S(2)}) copy-start(f32[4,128,512]{2,1,0:T(8,128)} %fusion.28) | copy-start | bytes 3145732
  60.1 5.6 %copy-start.2 = (bf16[2048,128]{1,0:T(8,128)(2,1)S(1)}, bf16[2048,128]{1,0:T(8,128)(2,1)}, u32[]{:S(2)}) copy-start(bf16[2048,128]{1,0:T(8,128)(2,1)} %param.7) | copy-start | bytes 1572868
  67.5 0.9 %copy-start.8 = (f32[128,128]{0,1:T(8,128)S(1)}, f32[128,128]{0,1:T(8,128)}, u32[]{:S(2)}) copy-start(f32[128,128]{0,1:T(8,128)} %fusion.11) | copy-start | bytes 196612
  69.5 0.8 %copy-start.7 = (f32[128,128]{1,0:T(8,128)S(1)}, f32[128,128]{1,0:T(8,128)}, u32[]{:S(2)}) copy-start(f32[128,128]{1,0:T(8,128)} %copy-done.6) | copy-start | bytes 196612
where the time goes:
time: 72 us; the launch traced here: 71.4 us
  blocking collectives  42.3 us (59%)
  matrix products  16.7 us (23%)
  local copies, waits for them, and re-layouts  7.31 us (10%)
  other arithmetic  4.29 us (6%)
  between operations  0.84 us (1%)
    psum x1, blocking collectives, body(): lax.psum((jnp.sum(output * output, (2, 3)), jnp.sum(scaled * output, (2,...  19 us
    all_gather x1, blocking collectives, body(): piece = lax.all_gather(totals[None], 'seq', axis=0, tiled=True)  12.4 us
    all_gather x1, blocking collectives, body(): piece = lax.all_gather(grad_total[None], 'seq', axis=0, tiled=True)  11 us
    another operation x1, other arithmetic  2.8 us
    dot_general x1, matrix products, body(): jnp.einsum('bthd,bhde->bthe', query4, prefix16, preferred_element_type=jn...  2.79 us
    convert_element_type x1, local copies, waits for them, and re-layouts, body(): value_grad.astype(jnp.bfloat16).reshape(tokens_here, -1)  2.04 us
    dot_general x1, matrix products, body(): jnp.einsum('bshd,bhde->bshe', key4, suffix16, preferred_element_type=jnp....  1.94 us
    dot_general x1, matrix products, body(): jnp.einsum('bthd,bshd->bhts', query4, key4, preferred_element_type=jnp.fl...  1.88 us

commit v1 on v0

--- a/solution.py
+++ b/solution.py
@@ -5,6 +5,25 @@
 
 HEAD_DIM = 128
 BLOCK = 512
+
+
+def collect(x, axis, dim):
+    size, index, span = (lax.axis_size(axis), lax.axis_index(axis), x.shape[dim])
+    right = [(i, (i + 1) % size) for i in range(size)]
+    backward = [(i, (i - 1) % size) for i in range(size)]
+    out = jnp.zeros((*x.shape[:dim], size * span, *x.shape[dim + 1 :]), x.dtype)
+    out = lax.dynamic_update_slice_in_dim(out, x, index * span, axis=dim)
+    from_left = from_right = x
+    half = size // 2
+    for lap in range(1, half + 1):
+        from_left = lax.ppermute(from_left, axis, right)
+        out = lax.dynamic_update_slice_in_dim(out, from_left, (index - lap) % size * span, axis=dim)
+        if lap < size - half:
+            from_right = lax.ppermute(from_right, axis, backward)
+            out = lax.dynamic_update_slice_in_dim(
+                out, from_right, (index + lap) % size * span, axis=dim
+            )
+    return out
 
 
 def causal_mask(size):
@@ -26,7 +45,7 @@
     position = lax.axis_index("seq")
     states = jnp.einsum("bshd,bshe->bhde", key4, value4, preferred_element_type=jnp.float32)
     totals = jnp.sum(states, 0)
-    piece = lax.all_gather(totals[None], "seq", axis=0, tiled=True)
+    piece = collect(totals[None], "seq", 0)
     anchor = jnp.arange(piece.shape[0], dtype=jnp.int32)
     keep = (anchor < position)[:, None, None, None]
     earlier = jnp.sum(jnp.where(keep, piece, 0.0), 0)

time: 72 us -> 89.2 us (1.24)
  local copies, waits for them, and re-layouts: 7.31 us -> 21.2 us
  blocking collectives: 42.3 us -> 30.6 us
  starting transfers between devices: 0 us -> 9.04 us
  matrix products: 16.7 us -> 19.7 us
  waiting for transfers between devices: 0 us -> 2.19 us
    all_gather x1 -> x0, blocking collectives: 12.4 us -> none  [body(): piece = lax.all_gather(totals[None], 'seq', axis=0, tiled=True)]
    dynamic_update_slice x0 -> x8, local copies, waits for them, and re-layouts: none -> 11.5 us  [the longest x4 5.74 us: collect(): lax.dynamic_update_slice_in_dim(out, from_left, (index - lap) % size * sp...]
    ppermute x0 -> x7, starting transfers between devices: none -> 9.04 us  [the longest x3 8.52 us: collect(): from_right = lax.ppermute(from_right, axis, backward)]
    ppermute x0 -> x7, local copies, waits for them, and re-layouts: none -> 4.81 us  [the longest x4 2.87 us: collect(): from_left = lax.ppermute(from_left, axis, right)]
    ppermute x0 -> x7, waiting for transfers between devices: none -> 2.19 us  [the longest x3 1.92 us: collect(): from_right = lax.ppermute(from_right, axis, backward)]
    slice x2, local copies, waits for them, and re-layouts: 1.63 us -> 0.03 us  [body(): after = jnp.concatenate([behind[1:], jnp.zeros_like(grad_states[:1])], 0)]
    all_gather x1 -> x0, local copies, waits for them, and re-layouts: 1.27 us -> none  [body(): piece = lax.all_gather(totals[None], 'seq', axis=0, tiled=True)]
    dot_general x1, matrix products: 1.09 us -> 2.35 us  [body(): jnp.einsum('bshe,bhde->bshd', value4, suffix16, preferred_element_type=jn...]
  transfers between devices with their start and end apart: 0 -> 7, of which waited for: 0 -> 2; matrix products, arithmetic and copies ran while one was open for 0% -> 20% of each run, Pallas kernels for 0% -> 0%
where the time goes in v1:
time: 89.2 us; the launch traced here: 88.6 us
  blocking collectives  30.6 us (34%)
  local copies, waits for them, and re-layouts  21.2 us (24%)
  matrix products  19.7 us (22%)
  starting transfers between devices  9.04 us (10%)
  other arithmetic  4.77 us (5%)
  waiting for transfers between devices  2.19 us (2%)
  between operations  1.16 us (1%)
    psum x1, blocking collectives, body(): lax.psum((jnp.sum(output * output, (2, 3)), jnp.sum(scaled * output, (2,...  19.7 us
    all_gather x1, blocking collectives, body(): piece = lax.all_gather(grad_total[None], 'seq', axis=0, tiled=True)  10.9 us
    ppermute x3, starting transfers between devices, collect(): from_right = lax.ppermute(from_right, axis, backward)  8.52 us
    dynamic_update_slice x4, local copies, waits for them, and re-layouts, collect(): lax.dynamic_update_slice_in_dim(out, from_left, (index - lap) % size * sp...  5.74 us
    dynamic_update_slice x3, local copies, waits for them, and re-layouts, collect(): lax.dynamic_update_slice_in_dim(out, from_right, (index + lap) % size * s...  4.31 us
    ppermute x4, local copies, waits for them, and re-layouts, collect(): from_left = lax.ppermute(from_left, axis, right)  2.87 us
    another operation x1, other arithmetic  2.8 us
    dot_general x1, matrix products, body(): jnp.einsum('bthd,bhde->bthe', query4, prefix16, preferred_element_type=jn...  2.8 us
  transfers between devices with their start and end apart: 7, of which 2 were waited for; matrix products, arithmetic and copies ran while one was open for 20% of the time, Pallas kernels for 0%

profile of v1, /device:TPU:0, one launch (start us, length us, event | category | flops | bytes accessed | tf_op | source)
XLA Modules:
  0.0 88.6 jit_solution(16194354359336651389)
XLA Ops:
  0.6 0.0 copy-start
  0.6 1.6 %fusion.26 = (f32[128,128]{1,0:T(8,128)S(1)}, f32[4,128,128]{2,1,0:T(8,128)S(1)}) fusion(bf16[4,512,128]{2,1,0:T(8,128)(2,1)} %bitcast.85, bf16[4,512,128]{2,1,0:T(8,128)(2,1)} %bitcast.89), kind=kOutput, calls=%fused_computation.45 | convolution fusion | flops 67158016 | bytes 1376256 | tf_op jit(solution)/shard_map/bshd,bshe->bhde/dot_general | solution.py:46
  2.3 0.5 collective-permute-start
  2.8 2.9 %collective-permute-start.1 = (f32[1,1,128,128]{3,2,1,0:T(8,128)S(1)}, f32[1,1,128,128]{3,2,1,0:T(8,128)S(1)}, u32[]{:S(2)}, u32[]{:S(2)}) collective-permute-start(f32[1,1,128,128]{3,2,1,0:T(8,128)S(1)} %bitcast.100), channel_id=1, source_target_pairs={{0,28},{4,0},{8,4},{12,8},{16,12},{20,16},{24,20},{28,24},{1,29},{... | collective-permute-start | bytes 196616 | tf_op jit(solution)/shard_map/ppermute | solution.py:22
  5.7 0.1 iota_compare_fusion
  5.8 1.9 %select_convert_fusion.1 = bf16[4,512,512]{2,1,0:T(8,128)(2,1)S(1)} fusion(bf16[4,512,128]{2,1,0:T(8,128)(2,1)S(1)} %bitcast.81, bf16[4,512,128]{2,1,0:T(8,128)(2,1)} %bitcast.86, pred[512,512]{1,0:T(8,128)(4,1)S(1)} %iota_compare_fusion), kind=kOutput, calls=%fused_computation.1 | convolution fusion | flops 270532608 | bytes 3407872 | tf_op jit(solution)/shard_map/bthd,bshd->bhts/dot_general | solution.py:55
  7.7 1.7 %convolution_bitcast_fusion.2 = f32[4,128,512]{1,2,0:T(8,128)} fusion(bf16[4,512,512]{2,1,0:T(8,128)(2,1)S(1)} %select_convert_fusion.1, bf16[4,512,128]{2,1,0:T(8,128)(2,1)S(1)} %bitcast.90), kind=kOutput, calls=%fused_computation.4 | convolution fusion | flops 268435456 | bytes 3670016 | tf_op jit(solution)/shard_map/bhts,bshe->bthe/dot_general | solution.py:57
  9.4 0.2 fusion.14
  9.6 0.1 copy.39
  9.9 1.4 %dynamic_update_slice.24 = f32[8,1,128,128]{2,0,3,1:T(8,128)S(1)} dynamic-update-slice(f32[8,1,128,128]{2,0,3,1:T(8,128)S(1)} %broadcast_in_dim.53, f32[1,1,128,128]{2,0,3,1:T(1,128)S(1)} %copy.39, s32[]{:T(128)S(6)} %select_n.72, s32[]{:T(128)} %constant.61.clone.1, s32[]{:T(128)} %constant.61.clone.1, s32[]{:T(128)} %constant.61.clone.1) | dynamic-update-slice | bytes 131076 | tf_op jit(solution)/shard_map/dynamic_update_slice | solution.py:15
  11.4 2.7 %collective-permute-start.3 = (f32[1,1,128,128]{3,2,1,0:T(8,128)S(1)}, f32[1,1,128,128]{3,2,1,0:T(8,128)}, u32[]{:S(2)}, u32[]{:S(2)}) collective-permute-start(f32[1,1,128,128]{3,2,1,0:T(8,128)S(1)} %collective-permute-done.1), channel_id=1, source_target_pairs={{0,28},{4,0},{8,4},{12,8},{16,12},{20,16},{24,20},{28,24},{1,29},{... | collective-permute-start | bytes 196616 | tf_op jit(solution)/shard_map/ppermute | solution.py:22
  14.1 0.3 collective-permute-done.2
  14.3 1.9 %collective-permute-done.3 = f32[1,1,128,128]{3,2,1,0:T(8,128)} collective-permute-done((f32[1,1,128,128]{3,2,1,0:T(8,128)S(1)}, f32[1,1,128,128]{3,2,1,0:T(8,128)}, u32[]{:S(2)}, u32[]{:S(2)}) %collective-permute-start.3) | collective-permute-done | bytes 65568 | tf_op jit(solution)/shard_map/ppermute | solution.py:22
  16.3 2.9 %collective-permute-start.5 = (f32[1,1,128,128]{3,2,1,0:T(8,128)}, f32[1,1,128,128]{3,2,1,0:T(8,128)}, u32[]{:S(2)}, u32[]{:S(2)}) collective-permute-start(f32[1,1,128,128]{3,2,1,0:T(8,128)} %collective-permute-done.3), channel_id=1, source_target_pairs={{0,28},{4,0},{8,4},{12,8},{16,12},{20,16},{24,20},{28,24},{1,29},{... | collective-permute-start | bytes 196616 | tf_op jit(solution)/shard_map/ppermute | solution.py:22
  19.2 0.9 %copy.40 = f32[1,1,128,128]{2,0,3,1:T(1,128)S(1)} copy(f32[1,1,128,128]{3,2,1,0:T(8,128)} %collective-permute-done) | data formatting | bytes 131072 | tf_op jit(solution)/shard_map/ppermute | solution.py:19
  20.1 1.4 %dynamic_update_slice.25 = f32[8,1,128,128]{2,0,3,1:T(8,128)S(1)} dynamic-update-slice(f32[8,1,128,128]{2,0,3,1:T(8,128)S(1)} %dynamic_update_slice.24, f32[1,1,128,128]{2,0,3,1:T(1,128)S(1)} %copy.40, s32[]{:T(128)S(6)} %select_n.74, s32[]{:T(128)} %constant.61.clone.1, s32[]{:T(128)} %constant.61.clone.1, s32[]{:T(128)} %constant.61.clone.1) | dynamic-update-slice | bytes 131076 | tf_op jit(solution)/shard_map/dynamic_update_slice | solution.py:20
  21.6 0.1 copy.41
  21.7 1.4 %dynamic_update_slice.26 = f32[8,1,128,128]{2,0,3,1:T(8,128)S(1)} dynamic-update-slice(f32[8,1,128,128]{2,0,3,1:T(8,128)S(1)} %dynamic_update_slice.25, f32[1,1,128,128]{2,0,3,1:T(1,128)S(1)} %copy.41, s32[]{:T(128)S(6)} %select_n.76, s32[]{:T(128)} %constant.61.clone.1, s32[]{:T(128)} %constant.61.clone.1, s32[]{:T(128)} %constant.61.clone.1) | dynamic-update-slice | bytes 131076 | tf_op jit(solution)/shard_map/dynamic_update_slice | solution.py:23
  23.1 0.9 %copy.42 = f32[1,1,128,128]{2,0,3,1:T(1,128)S(1)} copy(f32[1,1,128,128]{3,2,1,0:T(8,128)} %collective-permute-done.2) | data formatting | bytes 131072 | tf_op jit(solution)/shard_map/ppermute | solution.py:19
  24.0 1.4 %dynamic_update_slice.27 = f32[8,1,128,128]{2,0,3,1:T(8,128)S(1)} dynamic-update-slice(f32[8,1,128,128]{2,0,3,1:T(8,128)S(1)} %dynamic_update_slice.26, f32[1,1,128,128]{2,0,3,1:T(1,128)S(1)} %copy.42, s32[]{:T(128)S(6)} %select_n.78, s32[]{:T(128)} %constant.61.clone.1, s32[]{:T(128)} %constant.61.clone.1, s32[]{:T(128)} %constant.61.clone.1) | dynamic-update-slice | bytes 131076 | tf_op jit(solution)/shard_map/dynamic_update_slice | solution.py:20
  25.5 0.9 %copy.43 = f32[1,1,128,128]{2,0,3,1:T(1,128)S(1)} copy(f32[1,1,128,128]{3,2,1,0:T(8,128)} %collective-permute-done.3) | data formatting | bytes 131072 | tf_op jit(solution)/shard_map/ppermute | solution.py:22
  26.4 1.4 %dynamic_update_slice.28 = f32[8,1,128,128]{2,0,3,1:T(8,128)S(1)} dynamic-update-slice(f32[8,1,128,128]{2,0,3,1:T(8,128)S(1)} %dynamic_update_slice.27, f32[1,1,128,128]{2,0,3,1:T(1,128)S(1)} %copy.43, s32[]{:T(128)S(6)} %select_n.80, s32[]{:T(128)} %constant.61.clone.1, s32[]{:T(128)} %constant.61.clone.1, s32[]{:T(128)} %constant.61.clone.1) | dynamic-update-slice | bytes 131076 | tf_op jit(solution)/shard_map/dynamic_update_slice | solution.py:23
  27.9 0.1 copy.44
  28.0 1.4 %dynamic_update_slice.29 = f32[8,1,128,128]{2,0,3,1:T(8,128)S(1)} dynamic-update-slice(f32[8,1,128,128]{2,0,3,1:T(8,128)S(1)} %dynamic_update_slice.28, f32[1,1,128,128]{2,0,3,1:T(1,128)S(1)} %copy.44, s32[]{:T(128)S(6)} %select_n.82, s32[]{:T(128)} %constant.61.clone.1, s32[]{:T(128)} %constant.61.clone.1, s32[]{:T(128)} %constant.61.clone.1) | dynamic-update-slice | bytes 131076 | tf_op jit(solution)/shard_map/dynamic_update_slice | solution.py:20
  29.4 0.9 %copy.45 = f32[1,1,128,128]{2,0,3,1:T(1,128)S(1)} copy(f32[1,1,128,128]{3,2,1,0:T(8,128)} %collective-permute-done.5) | data formatting | bytes 131072 | tf_op jit(solution)/shard_map/ppermute | solution.py:22
  30.3 1.4 %dynamic_update_slice.30 = f32[8,1,128,128]{2,0,3,1:T(8,128)S(1)} dynamic-update-slice(f32[8,1,128,128]{2,0,3,1:T(8,128)S(1)} %dynamic_update_slice.29, f32[1,1,128,128]{2,0,3,1:T(1,128)S(1)} %copy.45, s32[]{:T(128)S(6)} %select_n.84, s32[]{:T(128)} %constant.61.clone.1, s32[]{:T(128)} %constant.61.clone.1, s32[]{:T(128)} %constant.61.clone.1) | dynamic-update-slice | bytes 131076 | tf_op jit(solution)/shard_map/dynamic_update_slice | solution.py:23
  31.8 0.9 %copy.46 = f32[1,1,128,128]{2,0,3,1:T(1,128)S(1)} copy(f32[1,1,128,128]{3,2,1,0:T(8,128)} %collective-permute-done.6) | data formatting | bytes 131072 | tf_op jit(solution)/shard_map/ppermute | solution.py:19
  32.7 1.4 %dynamic_update_slice.31 = f32[8,1,128,128]{2,0,3,1:T(8,128)S(1)} dynamic-update-slice(f32[8,1,128,128]{2,0,3,1:T(8,128)S(1)} %dynamic_update_slice.30, f32[1,1,128,128]{2,0,3,1:T(1,128)S(1)} %copy.46, s32[]{:T(128)S(6)} %select_n.86, s32[]{:T(128)} %constant.61.clone.1, s32[]{:T(128)} %constant.61.clone.1, s32[]{:T(128)} %constant.61.clone.1) | dynamic-update-slice | bytes 131076 | tf_op jit(solution)/shard_map/dynamic_update_slice | solution.py:20
  34.2 0.2 select_reduce_fusion
  34.4 0.1 copy.47
  34.5 2.8 %fusion.9 = (f32[4,512]{1,0:T(4,128)S(1)}, f32[4,512]{1,0:T(4,128)S(1)}, f32[4,512,1,128]{3,1,0,2:T(8,128)}) fusion(bf16[4,512,1,128]{3,1,0,2:T(8,128)(2,1)} %bitcast.94, f32[128]{0:T(128)S(1)} %copy-done.10, f32[4,128,512]{1,2,0:T(8,128)} %convolution_bitcast_fusion.2, bf16[4,512,128]{2,1,0:T(8,128)(2,1)S(1)} %bitcast.82, ...), kind=kOutput, calls=%fused_computation.20 | convolution fusion | flops 69070848 | bytes 3424768 | tf_op jit(solution)/shard_map/bthd,bhde->bthe/dot_general | solution.py:58
  37.3 19.7 %all-reduce.2 = (f32[4,512]{1,0:T(4,128)S(1)}, f32[4,512]{1,0:T(4,128)S(1)}) all-reduce(f32[4,512]{1,0:T(4,128)S(1)} %get-tuple-element.5, f32[4,512]{1,0:T(4,128)S(1)} %get-tuple-element.4), channel_id=1, replica_groups=mesh['seq'=8,'head'=4] {'head'}, use_global_device_ids=true, to_apply=%region_4.5 | all-reduce | flops 4096 | bytes 32768 | tf_op jit(solution)/shard_map/psum | solution.py:63
  57.0 2.8 %fusion.10 = (bf16[4,512,128]{2,1,0:T(8,128)(2,1)S(1)}, bf16[4,512,1,128]{3,1,0,2:T(8,128)(2,1)}) fusion(f32[4,512,1,128]{3,1,0,2:T(8,128)} %get-tuple-element.14, f32[4,512]{1,0:T(4,128)S(1)} %get-tuple-element.17, f32[4,512]{1,0:T(4,128)S(1)} %get-tuple-element.10, f32[128]{0:T(128)S(1)} %copy-done.10, f32[4,512]{1,0:T(4,128)S(1)} %get-tuple-element.11, ...), kind=kLoop, calls=%fused_computation.24 | loop fusion | flops 2621440 | bytes 2646528 | tf_op jit(solution)/shard_map/reshape.36
  59.8 1.5 %fusion.28 = f32[4,128,512]{2,1,0:T(8,128)} fusion(bf16[4,512,128]{2,1,0:T(8,128)(2,1)S(1)} %get-tuple-element.8, bf16[4,512,512]{2,1,0:T(8,128)(2,1)S(1)} %select_convert_fusion.1), kind=kOutput, calls=%fused_computation.47 | convolution fusion | flops 268435456 | bytes 3670016 | tf_op jit(solution)/shard_map/bhts,bthe->bshe/dot_general | solution.py:89
  61.4 1.1 %fusion.27 = (f32[128,128]{0,1:T(8,128)S(1)}, f32[4,128,128]{1,2,0:T(8,128)}) fusion(bf16[4,512,128]{2,1,0:T(8,128)(2,1)S(1)} %get-tuple-element.8, bf16[4,512,128]{2,1,0:T(8,128)(2,1)S(1)} %bitcast.84), kind=kOutput, calls=%fused_computation.46 | convolution fusion | flops 67158016 | bytes 1376256 | tf_op jit(solution)/shard_map/bthd,bthe->bhde/dot_general | solution.py:70
  62.4 0.8 select_convert_fusion
  63.2 1.9 %convolution_bitcast_fusion = f32[4,128,512]{1,2,0:T(8,128)} fusion(bf16[4,512,512]{2,1,0:T(8,128)(2,1)S(1)} %select_convert_fusion, bf16[4,512,128]{2,1,0:T(8,128)(2,1)S(1)} %bitcast.83), kind=kOutput, calls=%fused_computation.2 | convolution fusion | flops 268435456 | bytes 3670016 | tf_op jit(solution)/shard_map/bhts,bthd->bshd/dot_general | solution.py:85
  65.1 0.7 convolution_bitcast_fusion.1
  65.8 10.9 %all-gather = f32[1024,128]{0,1:T(8,128)S(1)} all-gather(f32[128,128]{0,1:T(8,128)S(1)} %get-tuple-element.15), channel_id=2, replica_groups=mesh['seq'=8,'head'=4] {'seq'}, dimensions={0}, use_global_device_ids=true | all-gather | bytes 589824 | tf_op jit(solution)/shard_map/all_gather | solution.py:72
  76.7 0.9 %copy.66 = f32[16,8,8,128]{3,2,1,0:T(8,128)} copy(f32[16,8,8,128]{3,1,2,0:T(8,128)S(1)} %bitcast.93) | data formatting | bytes 1048576
  77.6 1.0 %reverse.4 = f32[4,128,128]{1,2,0:T(8,128)S(1)} reverse(f32[4,128,128]{1,2,0:T(8,128)} %get-tuple-element.16), dimensions={0} | reverse | bytes 524288 | tf_op jit(solution)/shard_map/reverse
  78.6 0.2 fusion.12
  78.8 1.3 %fusion.11 = f32[128,128]{0,1:T(8,128)S(1)} fusion(f32[16,8,8,128]{3,2,1,0:T(8,128)} %copy.66, pred[8]{0:T(512)(128)(4,1)S(1)} %iota_compare_fusion.1), kind=kLoop, calls=%fused_computation.26 | loop fusion | flops 245760 | bytes 589832 | tf_op jit(solution)/shard_map/reduce_sum | solution.py:75
  80.1 0.6 copy-done.7
  80.8 2.3 %fusion.4 = bf16[4,512,1,128]{1,3,0,2:T(8,128)(2,1)} fusion(f32[4,128,512]{2,1,0:T(8,128)} %fusion.28, bf16[4,512,128]{2,1,0:T(8,128)(2,1)S(1)} %bitcast.88, f32[3,1,128,128]{2,3,0,1:T(8,128)S(1)} %slice.11, f32[128,128]{0,1:T(8,128)S(1)} %fusion.11), kind=kOutput, calls=%fused_computation.13 | convolution fusion | flops 67764224 | bytes 2359296 | tf_op jit(solution)/shard_map/bshd,bhde->bshe/dot_general | solution.py:90
  83.1 2.1 %copy.56 = bf16[4,512,1,128]{3,1,0,2:T(8,128)(2,1)} copy(bf16[4,512,1,128]{1,3,0,2:T(8,128)(2,1)} %fusion.4) | data formatting | bytes 1048576 | tf_op jit(solution)/shard_map/convert_element_type | solution.py:97
  85.1 2.3 %fusion.3 = bf16[4,128,512]{1,2,0:T(8,128)(2,1)} fusion(f32[4,128,512]{1,2,0:T(8,128)} %convolution_bitcast_fusion, bf16[4,512,128]{2,1,0:T(8,128)(2,1)S(1)} %bitcast.92, f32[3,1,128,128]{2,3,0,1:T(8,128)S(1)} %slice.11, f32[128,128]{0,1:T(8,128)} %copy-done.7), kind=kOutput, calls=%fused_computation.12 | convolution fusion | flops 67764224 | bytes 2359296 | tf_op jit(solution)/shard_map/bshe,bhde->bshd/dot_general | solution.py:86
  87.5 1.1 %fusion.1 = bf16[4,128,512]{1,2,0:T(8,128)(2,1)} fusion(f32[4,128,512]{1,2,0:T(8,128)S(1)} %convolution_bitcast_fusion.1, bf16[4,512,128]{2,1,0:T(8,128)(2,1)S(1)} %get-tuple-element.8, f32[3,1,128,128]{3,2,0,1:T(8,128)S(1)} %slice.12, f32[128,128]{1,0:T(8,128)S(1)} %copy-done.6), kind=kOutput, calls=%fused_computation.10 | convolution fusion | flops 67764224 | bytes 2359296 | tf_op jit(solution)/shard_map/bthe,bhde->bthd/dot_general | solution.py:82
  (35 shorter events, 0.2 us)
Async XLA Ops:
  0.6 5.2 %copy-start = (bf16[2048,128]{1,0:T(8,128)(2,1)S(1)}, bf16[2048,128]{1,0:T(8,128)(2,1)}, u32[]{:S(2)}) copy-start(bf16[2048,128]{1,0:T(8,128)(2,1)} %param.5) | copy-start | bytes 1572868
  2.3 5.5 %copy-start.2 = (bf16[2048,128]{1,0:T(8,128)(2,1)S(1)}, bf16[2048,128]{1,0:T(8,128)(2,1)}, u32[]{:S(2)}) copy-start(bf16[2048,128]{1,0:T(8,128)(2,1)} %param.7) | copy-start | bytes 1572868
  2.3 7.2 %collective-permute-start = (f32[1,1,128,128]{3,2,1,0:T(8,128)S(1)}, f32[1,1,128,128]{3,2,1,0:T(8,128)}, u32[]{:S(2)}, u32[]{:S(2)}) collective-permute-start(f32[1,1,128,128]{3,2,1,0:T(8,128)S(1)} %bitcast.99), channel_id=1, source_target_pairs={{0,4},{4,8},{8,12},{12,16},{16,20},{20,24},{24,28},{28,0},{1,5},{5... | collective-permute-start | bytes 196616 | tf_op jit(solution)/shard_map/ppermute | solution.py:19
  2.8 8.6 %collective-permute-start.1 = (f32[1,1,128,128]{3,2,1,0:T(8,128)S(1)}, f32[1,1,128,128]{3,2,1,0:T(8,128)S(1)}, u32[]{:S(2)}, u32[]{:S(2)}) collective-permute-start(f32[1,1,128,128]{3,2,1,0:T(8,128)S(1)} %bitcast.100), channel_id=1, source_target_pairs={{0,28},{4,0},{8,4},{12,8},{16,12},{20,16},{24,20},{28,24},{1,29},{... | collective-permute-start | bytes 196616 | tf_op jit(solution)/shard_map/ppermute | solution.py:22
  5.8 3.6 %copy-start.8 = (pred[512,512]{1,0:T(8,128)(4,1)}, pred[512,512]{1,0:T(8,128)(4,1)S(1)}, u32[]{:S(2)}) copy-start(pred[512,512]{1,0:T(8,128)(4,1)S(1)} %iota_compare_fusion) | copy-start | bytes 786436
  9.4 4.9 %collective-permute-start.2 = (f32[1,1,128,128]{3,2,1,0:T(8,128)}, f32[1,1,128,128]{3,2,1,0:T(8,128)}, u32[]{:S(2)}, u32[]{:S(2)}) collective-permute-start(f32[1,1,128,128]{3,2,1,0:T(8,128)} %collective-permute-done), channel_id=1, source_target_pairs={{0,4},{4,8},{8,12},{12,16},{16,20},{20,24},{24,28},{28,0},{1,5},{5... | collective-permute-start | bytes 196616 | tf_op jit(solution)/shard_map/ppermute | solution.py:19
  9.6 24.9 %copy-start.10 = (f32[128]{0:T(128)S(1)}, f32[128]{0:T(128)}, u32[]{:S(2)}) copy-start(f32[128]{0:T(128)} %param.8) | copy-start | bytes 1540
  11.4 4.9 %collective-permute-start.3 = (f32[1,1,128,128]{3,2,1,0:T(8,128)S(1)}, f32[1,1,128,128]{3,2,1,0:T(8,128)}, u32[]{:S(2)}, u32[]{:S(2)}) collective-permute-start(f32[1,1,128,128]{3,2,1,0:T(8,128)S(1)} %collective-permute-done.1), channel_id=1, source_target_pairs={{0,28},{4,0},{8,4},{12,8},{16,12},{20,16},{24,20},{28,24},{1,29},{... | collective-permute-start | bytes 196616 | tf_op jit(solution)/shard_map/ppermute | solution.py:22
  14.3 4.8 %collective-permute-start.4 = (f32[1,1,128,128]{3,2,1,0:T(8,128)}, f32[1,1,128,128]{3,2,1,0:T(8,128)S(1)}, u32[]{:S(2)}, u32[]{:S(2)}) collective-permute-start(f32[1,1,128,128]{3,2,1,0:T(8,128)} %collective-permute-done.2), channel_id=1, source_target_pairs={{0,4},{4,8},{8,12},{12,16},{16,20},{20,24},{24,28},{28,0},{1,5},{5... | collective-permute-start | bytes 196616 | tf_op jit(solution)/shard_map/ppermute | solution.py:19
  16.3 13.1 %collective-permute-start.5 = (f32[1,1,128,128]{3,2,1,0:T(8,128)}, f32[1,1,128,128]{3,2,1,0:T(8,128)}, u32[]{:S(2)}, u32[]{:S(2)}) collective-permute-start(f32[1,1,128,128]{3,2,1,0:T(8,128)} %collective-permute-done.3), channel_id=1, source_target_pairs={{0,28},{4,0},{8,4},{12,8},{16,12},{20,16},{24,20},{28,24},{1,29},{... | collective-permute-start | bytes 196616 | tf_op jit(solution)/shard_map/ppermute | solution.py:22
  19.2 12.6 %collective-permute-start.6 = (f32[1,1,128,128]{3,2,1,0:T(8,128)S(1)}, f32[1,1,128,128]{3,2,1,0:T(8,128)}, u32[]{:S(2)}, u32[]{:S(2)}) collective-permute-start(f32[1,1,128,128]{3,2,1,0:T(8,128)S(1)} %collective-permute-done.4), channel_id=1, source_target_pairs={{0,4},{4,8},{8,12},{12,16},{16,20},{20,24},{24,28},{28,0},{1,5},{5... | collective-permute-start | bytes 196616 | tf_op jit(solution)/shard_map/ppermute | solution.py:19
  34.5 22.5 %copy-start.5 = (f32[128,128]{1,0:T(8,128)}, f32[128,128]{1,0:T(8,128)S(1)}, u32[]{:S(2)}) copy-start(f32[128,128]{1,0:T(8,128)S(1)} %copy.47) | copy-start | bytes 196612
  59.8 2.6 %copy-start.3 = (bf16[2048,128]{1,0:T(8,128)(2,1)S(1)}, bf16[2048,128]{1,0:T(8,128)(2,1)}, u32[]{:S(2)}) copy-start(bf16[2048,128]{1,0:T(8,128)(2,1)} %param.7) | copy-start | bytes 1572868
  59.8 2.6 %copy-start.9 = (pred[512,512]{1,0:T(8,128)(4,1)S(1)}, pred[512,512]{1,0:T(8,128)(4,1)}, u32[]{:S(2)}) copy-start(pred[512,512]{1,0:T(8,128)(4,1)} %copy-done.8) | copy-start | bytes 786436
  63.2 1.9 %copy-start.1 = (bf16[2048,128]{1,0:T(8,128)(2,1)S(1)}, bf16[2048,128]{1,0:T(8,128)(2,1)}, u32[]{:S(2)}) copy-start(bf16[2048,128]{1,0:T(8,128)(2,1)} %param.6) | copy-start | bytes 1572868
  78.8 6.3 %copy-start.4 = (bf16[2048,128]{1,0:T(8,128)(2,1)S(1)}, bf16[2048,128]{1,0:T(8,128)(2,1)}, u32[]{:S(2)}) copy-start(bf16[2048,128]{1,0:T(8,128)(2,1)} %param.7) | copy-start | bytes 1572868
  80.1 0.6 copy-start.7
  83.1 4.4 %copy-start.6 = (f32[128,128]{1,0:T(8,128)S(1)}, f32[128,128]{1,0:T(8,128)}, u32[]{:S(2)}) copy-start(f32[128,128]{1,0:T(8,128)} %copy-done.5) | copy-start | bytes 196612
